TPU v7x, 128 devices: a whole 4x4x4 slice. The times are simulated.
128 devices in a mesh: panel: 32 (over y, z_lo, x), pole: 4 (over z_hi, core).
Axes of the slice: x: 4, y: 4, z: 4 (z_hi: 2, z_lo: 2; z = z_hi * 2 + z_lo), core: 2. Of those that a mesh axis runs over, the one named last changes fastest.
Arguments:
- amplitudes: bfloat16 [10240, 4096], P('panel', 'pole'), may hold values from -0.75 to 0.75
- factors: float32 [2, 4096], P(None, 'pole'), may hold values from -2 to 2
Outputs:
- rmatrix: float32 [2, 10240, 10240], P(None, 'panel', 'pole')
All inputs are finite; a program needn't handle non-finite values.
Results may differ from a plain program's by a relative error of at most 0.0029.
Values may be sent and summed in bfloat16 or wider, within the bound.
A program may use at most 128 MiB of HBM per device.

v0:
```python
import jax
import jax.numpy as jnp
from jax import lax
from jax.sharding import PartitionSpec as P


def shards(amplitudes, factors):
    energies = factors.shape[0]
    rows = amplitudes.shape[0]
    scaled = (factors[:, None, :] * amplitudes[None, :, :].astype(jnp.float32)).astype(jnp.bfloat16)
    scaled = scaled.reshape(energies * rows, amplitudes.shape[1])
    piece = lax.all_gather(amplitudes, "panel", axis=0, tiled=True)
    block = lax.dot_general(
        scaled, piece, (((1,), (1,)), ((), ())), preferred_element_type=jnp.float32
    )
    partial_block = block.reshape(energies, rows, piece.shape[0])
    return lax.psum_scatter(partial_block, "pole", scatter_dimension=2, tiled=True)


def solution(mesh):
    in_specs = (P("panel", "pole"), P(None, "pole"))
    out_specs = P(None, "panel", "pole")
    return jax.shard_map(shards, mesh=mesh, in_specs=in_specs, out_specs=out_specs, check_vma=False)
```

profile of v0, /device:TPU:16, one launch (start us, length us, event | category | flops | bytes accessed | tf_op | source)
XLA Modules:
  0.0 466.6 jit_solution(860446229407065755)
XLA Ops:
  6.5 0.0 all-gather.2.cloned.1.call-start
  6.5 0.7 all-gather.2.cloned.1.call-update
  7.3 0.0 reduce-scatter.2.cloned.1.call-start
  7.3 1.2 convert_element_type.9
  8.5 234.7 %all-gather.2.cloned.1.call-done = bf16[10240,1024]{1,0:T(8,128)(2,1)} async-done(((bf16[320,1024]{1,0:T(8,128)(2,1)}), bf16[10240,1024]{1,0:T(8,128)(2,1)}) %all-gather.2.cloned.1.call-update) | async-done | bytes 20971536 | tf_op jit(solution)/shard_map/all_gather | solution.py:12
  243.2 23.0 %fusion = f32[2,320,10240]{2,1,0:T(8,128)} fusion(bf16[10240,1024]{1,0:T(8,128)(2,1)} %all-gather.2.cloned.1.call-done, f32[320,1024]{1,0:T(8,128)S(1)} %convert_element_type.9, f32[2,1024]{1,0:T(2,128)} %param.3), kind=kOutput, calls=%fused_computation | convolution fusion | flops 13423083520 | bytes 48504832 | tf_op jit(solution)/shard_map/dot_general | solution.py:13
  266.2 0.0 reduce-scatter.2.cloned.1.call-update
  266.2 193.5 %reduce-scatter.2.cloned.1.call-done = f32[2,320,2560]{2,1,0:T(8,128)} async-done(((f32[2,320,10240]{2,1,0:T(8,128)}), f32[2,320,2560]{2,1,0:T(8,128)}) %reduce-scatter.2.cloned.1.call-update) | async-done | bytes 6553616 | tf_op jit(solution)/shard_map/reduce_scatter | solution.py:17
Async XLA Ops:
  6.5 236.6 %all-gather.2.cloned.1.call-start = ((), (), s32[]{:S(2)}) async-start(), calls=%async_computation.1 | async-start | bytes 21626880 | tf_op jit(solution)/shard_map/all_gather | solution.py:12
  7.3 452.5 %reduce-scatter.2.cloned.1.call-start = ((), (), s32[]{:S(2)}) async-start(), calls=%async_computation.2 | async-start | bytes 32768000 | tf_op jit(solution)/shard_map/reduce_scatter | solution.py:17
Sparse Core Ops, SparseCore 0:
  9.0 234.1 all-gather.1
  266.3 193.3 reduce-scatter.1
where the time goes:
time: 468 us; the launch traced here: 467 us
  waiting for transfers between devices  429 us (92%)
  matrix products  23 us (5%)
  between operations  13.4 us (3%)
    all_gather x1, waiting for transfers between devices, shards(): piece = lax.all_gather(amplitudes, 'panel', axis=0, tiled=True)  235 us
    reduce_scatter x1, waiting for transfers between devices, shards(): lax.psum_scatter(partial_block, 'pole', scatter_dimension=2, tiled=True)  194 us
    dot_general x1, matrix products, shards(): lax.dot_general(scaled, piece, (((1,), (1,)), ((), ())), preferred_elemen...  23 us
  transfers between devices with their start and end apart: 2, of which 2 were waited for; matrix products, arithmetic and copies ran while one was open for 0% of the time, Pallas kernels for 0%

commit v1 on v0

v1 whole, which is shorter than its diff:
```python
import jax
import jax.numpy as jnp
from jax import lax
from jax.experimental import pallas as pl
from jax.experimental.pallas import tpu as pltpu
from jax.sharding import PartitionSpec as P

MESH = pl.DeviceIdType.MESH
LAST = (((1,), (1,)), ((), ()))
XFIRST = (2, 3)

U = lambda j, ms, ts=(0, 1): [("U", j, t, m) for m in ms for t in ts]
SIDES = lambda ms, ts=(0, 1): [("U", j, t, m) for t in ts for m in ms for j in (3, 1)]
ORDER = (
    [("R", "s01"), ("U", 0, 0, 0), ("U", 0, 0, 1), ("R", "12_0"), ("R", "10_1"), ("U", 0, 1, 0), ("U", 0, 1, 1)]
    + [("U", 3, 0, 0), ("U", 1, 0, 0), ("R", "12_1"), ("R", "10_0"), ("U", 3, 0, 1), ("U", 1, 0, 1)]
    + [("R", "02"), ("S", 0), ("R", "s11"), ("S", 1), ("R", "s03"), ("R", "s13")]
    + [("U", 0, 0, 2), ("U", 0, 0, 3), ("U", 0, 1, 2), ("U", 0, 1, 3)]
    + [("U", 3, 1, 0), ("U", 1, 1, 0), ("U", 3, 1, 1), ("U", 1, 1, 1)]
    + [("S", 2), ("S", 3)]
    + [("U", 3, 0, 2), ("U", 1, 0, 2), ("U", 3, 0, 3), ("U", 1, 0, 3)]
    + [("U", 2, 0, 0), ("U", 2, 1, 0)]
    + [("U", 3, 1, 2), ("U", 1, 1, 2), ("U", 3, 1, 3), ("U", 1, 1, 3)]
    + [("U", 2, 0, 1), ("U", 2, 1, 1)]
    + [("U", 2, 0, 2), ("U", 2, 1, 2), ("U", 2, 0, 3), ("U", 2, 1, 3)]
)


class Sems:
    def __init__(self):
        self.ids = {}

    def __getitem__(self, name):
        return self.ids.setdefault(name, len(self.ids))


def kernel(names, a, f, outl, outr, rows, facs, scaled, cols, acc, snd, sems):
    p, q = lax.axis_index("panel"), lax.axis_index("pole")
    x, zl, y = lax.rem(p, 4), lax.rem(lax.div(p, 4), 2), lax.div(p, 8)
    zh, c = lax.div(q, 2), lax.rem(q, 2)
    half = a.shape[0] // 2

    def device(x, y, zl, zh, c):
        return ((y * 2 + zl) * 4 + x, zh * 2 + c)

    up = 2 * c - 1
    role = lax.rem((y - (2 * zh + c)) * up + 4, 4)
    right, left = device(lax.rem(x + 1, 4), y, zl, zh, c), device(lax.rem(x + 3, 4), y, zl, zh, c)
    ahead, behind = device(x, lax.rem(y + up + 4, 4), zl, zh, c), device(x, lax.rem(y - up + 4, 4), zl, zh, c)
    sibling = device(x, y, zl, zh, 1 - c)
    partner, other = device(x, y, 1 - zl, zh, c), device(x, y, 1 - zl, 1 - zh, c)
    across, across2 = device(x, y, zl, 1 - zh, c), device(x, y, zl, 1 - zh, 1 - c)

    sem = lambda name: sems.at[names[name]]

    def to_slot(src, dst, send_name, slot_name, to):
        return pltpu.make_async_remote_copy(
            src_ref=src, dst_ref=dst, send_sem=sem(("s",) + send_name), recv_sem=sem(("r",) + slot_name),
            device_id=to, device_id_type=MESH,
        )

    barrier = pltpu.get_barrier_semaphore()
    greeted = (right, left, ahead, behind, sibling, partner, other, across, across2)
    for to in greeted:
        pl.semaphore_signal(barrier, inc=1, device_id=to, device_id_type=MESH)
    pl.semaphore_wait(barrier, len(greeted))

    finish = []

    def start(make, when=None):
        if when is None:
            make().start()
            finish.append(lambda: make().wait_send())
        else:
            pl.when(when)(lambda: make().start())
            finish.append(lambda: pl.when(when)(lambda: make().wait_send()))

    part = lambda ref, t: ref.at[pl.ds(t * half, half)]

    def source(j, t, m, root):
        if root:
            return part(a, t) if m == 0 else part(rows.at[0, m], t)
        return cols.at[j, t, m]

    def sends(j, t, m):
        every = (0, 1, 2, 3)
        out = []
        xroles = (0,) if m in XFIRST else every
        if j == 0:
            out += [(xroles, right, 3), (xroles, left, 1)]
        elif j == 3 and t == 0:
            out += [(xroles, right, 2)]
        elif j == 1 and t == 1:
            out += [(xroles, left, 2)]
        if j == 0 or m in XFIRST:
            out += [((0, 1), ahead, j), ((0,), behind, j)]
        return out

    def forward(j, t, m):
        for n, (roles, to, slot) in enumerate(sends(j, t, m)):
            def make(root, to=to, slot=slot, n=n):
                return to_slot(source(j, t, m, root), cols.at[slot, t, m], ("c", j, t, m, n), ("c", slot, t, m), to)
            if j == 0:
                if 0 in roles:
                    start(lambda make=make: make(True), role == 0)
                rest = tuple(i for i in roles if i != 0)
                if rest:
                    start(lambda make=make: make(False), (role == 1) if rest == (1,) else (role != 0))
            elif len(roles) == 4:
                start(lambda make=make: make(False))
            else:
                start(lambda make=make: make(False), (role == 0) if roles == (0,) else (role < 2))

    def wait_unit(j, t, m):
        to_slot(cols.at[j, t, m], cols.at[j, t, m], ("c", 0, 0, 0, 0), ("c", j, t, m), right).wait_recv()

    def send_unit(j, t, m):
        if j == 0:
            def root_local():
                pltpu.make_async_copy(source(0, t, m, True), cols.at[0, t, m], sem(("l", t, m))).start()
            pl.when(role == 0)(root_local)
            pl.when(role != 0)(lambda: wait_unit(j, t, m))
        else:
            wait_unit(j, t, m)
        forward(j, t, m)

    def wait_rows(w, m, t=None):
        ref = rows.at[w, m] if t is None else part(rows.at[w, m], t)
        name = ("w", w, m) if t is None else ("w", w, m, t)
        to_slot(ref, ref, ("c", 0, 0, 0, 0), name, sibling).wait_recv()

    def to_sibling(w, m):
        src = a if (w, m) == (0, 0) else rows.at[w, m]
        start(lambda: to_slot(src, rows.at[w, m + 1], ("w", w, m), ("w", w, m + 1), sibling))

    def row_event(kind):
        if kind == "s01":
            wait_rows(0, 1)
        elif kind == "12_0":
            wait_rows(1, 2, 0)
            start(lambda: to_slot(part(rows.at[1, 2], 0), part(rows.at[0, 2], 0), ("z", 0), ("w", 0, 2, 0), partner))
        elif kind == "10_1":
            wait_rows(1, 0, 1)
            start(lambda: to_slot(part(rows.at[1, 0], 1), part(rows.at[0, 2], 1), ("z", 1), ("w", 0, 2, 1), other))
        elif kind == "12_1":
            wait_rows(1, 2, 1)
            to_sibling(1, 2)
        elif kind == "10_0":
            wait_rows(1, 0, 0)
            to_sibling(1, 0)
        elif kind == "02":
            wait_rows(0, 2, 0)
            wait_rows(0, 2, 1)
            to_sibling(0, 2)
        elif kind == "s11":
            wait_rows(1, 1)
        elif kind == "s03":
            wait_rows(0, 3)
        elif kind == "s13":
            wait_rows(1, 3)

    def scale(m):
        if m:
            to_slot(facs.at[m], facs.at[m], ("c", 0, 0, 0, 0), ("f", m), sibling).wait_recv()
        fac = f if m == 0 else facs.at[m]
        energies, full, step = f.shape[0], 2 * half, 32
        for w in (0, 1):
            src = a if (w, m) == (0, 0) else rows.at[w, m]

            def body(i, _):
                at = pl.ds(pl.multiple_of(i * step, step), step)
                block = src[at, :].astype(jnp.float32)
                for e in range(energies):
                    scaled[m, w * energies + e, at, :] = (block * fac[e : e + 1, :]).astype(jnp.bfloat16)
                return 0

            lax.fori_loop(0, full // step, body, 0)

    def piece(i, j, t, w, e):
        total = None
        for m in range(4):
            term = lax.dot_general(scaled[m, w * 2 + e], cols[j, t, m], LAST, preferred_element_type=jnp.float32)
            total = term if total is None else total + term
        if w:
            snd[i, e] = total.astype(jnp.bfloat16)
        else:
            acc[i, e] = total
        if e == 1:
            column = lax.rem(x + j, 4)
            if w:
                start(lambda: to_slot(snd.at[i], outr.at[column, t], ("o", i), ("o", j, t), partner))
            else:
                local = lambda: pltpu.make_async_copy(acc.at[i], outl.at[column, t], sem(("ol", i)))
                local().start()
                finish.append(lambda: local().wait())

    def z_start(t, m, to):
        start(lambda: to_slot(part(a, t), part(rows.at[1, m], t), ("z", m, t), ("w", 1, m, t), to))

    z_start(0, 2, other)
    z_start(1, 0, partner)
    to_sibling(0, 0)
    z_start(1, 2, other)
    z_start(0, 0, partner)
    for m, to in ((1, sibling), (2, across), (3, across2)):
        start(lambda m=m, to=to: to_slot(f, facs.at[m], ("f", m), ("f", m), to))

    pending, seen, done = [], {}, 0
    scaled_ready = 0
    ready = []
    for event in ORDER:
        if event[0] == "R":
            row_event(event[1])
        elif event[0] == "S":
            scale(event[1])
            scaled_ready += 1
        else:
            _, j, t, m = event
            send_unit(j, t, m)
            seen[j, t] = seen.get((j, t), 0) + 1
            if seen[j, t] == 4:
                ready.append((j, t))
        if scaled_ready == 4:
            while ready:
                j, t = ready.pop(0)
                if j == 0:
                    for m in range(4):
                        pl.when(role == 0)(
                            lambda: pltpu.make_async_copy(source(0, t, m, True), cols.at[0, t, m], sem(("l", t, m))).wait()
                        )
                pending += [(done, j, t, w, e) for w in (1, 0) for e in (0, 1)]
                done += 1
            if pending:
                piece(*pending.pop(0))
    while pending:
        piece(*pending.pop(0))

    for j in range(4):
        for t in (0, 1):
            column = lax.rem(x + j, 4)
            to_slot(snd.at[0], outr.at[column, t], ("o", 0), ("o", j, t), partner).wait_recv()
    for wait in finish:
        wait()


def gather_and_multiply(a, f):
    n, k = a.shape
    half = n // 2
    names = Sems()
    shape = (4, 2, 2, n, half)
    bf16, f32 = jnp.bfloat16, jnp.float32
    any_ = pl.BlockSpec(memory_space=pl.ANY)
    vmem = pl.BlockSpec(memory_space=pltpu.VMEM)
    return pl.pallas_call(
        lambda *refs: kernel(names, *refs),
        out_shape=(jax.ShapeDtypeStruct(shape, f32), jax.ShapeDtypeStruct(shape, bf16)),
        in_specs=[vmem, vmem],
        out_specs=(any_, any_),
        scratch_shapes=[
            pltpu.VMEM((2, 4, n, k), bf16),
            pltpu.VMEM((4, 2, k), f32),
            pltpu.VMEM((4, 4, n, k), bf16),
            pltpu.VMEM((4, 2, 4, half, k), bf16),
            pltpu.VMEM((8, 2, n, half), f32),
            pltpu.VMEM((8, 2, n, half), bf16),
            pltpu.SemaphoreType.DMA((256,)),
        ],
        compiler_params=pltpu.CompilerParams(
            collective_id=0, has_side_effects=True, vmem_limit_bytes=52 << 20
        ),
        cost_estimate=pl.CostEstimate(flops=2 * 4 * n * 8 * half * 4 * k, bytes_accessed=8 * n * n * 16, transcendentals=0),
        name="gather_multiply",
    )(a, f)


def shards(a, f):
    n = a.shape[0]
    zl = lax.rem(lax.div(lax.axis_index("panel"), 4), 2)
    mine, theirs = gather_and_multiply(a, f)

    def flat(block):
        return jnp.transpose(block, (2, 3, 0, 1, 4)).reshape(2, n, 4 * n)

    mine, theirs = flat(mine), flat(theirs).astype(jnp.float32)
    first = jnp.where(zl == 0, mine, theirs)
    second = jnp.where(zl == 0, theirs, mine)
    return jnp.concatenate([first, second], axis=2)


def solution(mesh):
    in_specs = (P("panel", "pole"), P(None, "pole"))
    out_specs = P(None, "panel", "pole")
    return jax.shard_map(shards, mesh=mesh, in_specs=in_specs, out_specs=out_specs, check_vma=False)
```

time: 468 us -> 172 us (0.37)
  waiting for transfers between devices: 429 us -> 0 us
  Pallas kernels: 0 us -> 134 us
  matrix products: 23 us -> 0 us
  local copies, waits for them, and re-layouts: 0 us -> 21.7 us
  other arithmetic: 1.22 us -> 15.5 us
  between operations: 13.4 us -> 0.01 us
    all_gather x1 -> x0, waiting for transfers between devices: 235 us -> none  [shards(): piece = lax.all_gather(amplitudes, 'panel', axis=0, tiled=True)]
    reduce_scatter x1 -> x0, waiting for transfers between devices: 194 us -> none  [shards(): lax.psum_scatter(partial_block, 'pole', scatter_dimension=2, tiled=True)]
    pallas_call x0 -> x1, Pallas kernels: none -> 134 us  [gather_and_multiply(): pl.pallas_call(lambda *refs: kernel(names, *refs), out_shape=(jax.ShapeDt...]
    dot_general x1 -> x0, matrix products: 23 us -> none  [shards(): lax.dot_general(scaled, piece, (((1,), (1,)), ((), ())), preferred_elemen...]
    select_n x0 -> x2, local copies, waits for them, and re-layouts: none -> 11.3 us  [the longest x1 5.67 us: shards(): first = jnp.where(zl == 0, mine, theirs)]
    select_n x0 -> x1, other arithmetic: none -> 8.63 us  [shards(): first = jnp.where(zl == 0, mine, theirs)]
    concatenate x0 -> x1, local copies, waits for them, and re-layouts: none -> 8.56 us  [shards(): return jnp.concatenate([first, second], axis=2)]
    concatenate x0 -> x1, other arithmetic: none -> 6.89 us  [shards(): return jnp.concatenate([first, second], axis=2)]
  transfers between devices with their start and end apart: 2 -> 0, of which waited for: 2 -> 0; matrix products, arithmetic and copies ran while one was open for 0% -> 0% of each run, Pallas kernels for 0% -> 0%
where the time goes in v1:
time: 172 us; the launch traced here: 171 us
  Pallas kernels  134 us (78%)
  local copies, waits for them, and re-layouts  21.7 us (13%)
  other arithmetic  15.5 us (9%)
    pallas_call x1, Pallas kernels, gather_and_multiply(): pl.pallas_call(lambda *refs: kernel(names, *refs), out_shape=(jax.ShapeDt...  134 us
    select_n x1, other arithmetic, shards(): first = jnp.where(zl == 0, mine, theirs)  8.63 us
    concatenate x1, local copies, waits for them, and re-layouts, shards(): return jnp.concatenate([first, second], axis=2)  8.56 us
    concatenate x1, other arithmetic, shards(): return jnp.concatenate([first, second], axis=2)  6.89 us
    select_n x1, local copies, waits for them, and re-layouts, shards(): first = jnp.where(zl == 0, mine, theirs)  5.67 us
    select_n x1, local copies, waits for them, and re-layouts, shards(): second = jnp.where(zl == 0, theirs, mine)  5.65 us

profile of v1, /device:TPU:16, one launch (start us, length us, event | category | flops | bytes accessed | tf_op | source)
XLA Modules:
  0.0 171.1 jit_solution(14866882246534992194)
XLA Ops:
  0.0 0.0 copy-start
  0.0 1.1 copy-done
  1.1 0.0 copy-start.1
  1.1 0.7 copy-done.1
  1.8 133.9 %gather_multiply.1 = (f32[4,2,2,320,160]{4,3,2,1,0:T(8,128)}, bf16[4,2,2,320,160]{4,3,2,1,0:T(8,128)(2,1)}) custom-call(bf16[320,1024]{1,0:T(8,128)(2,1)S(1)} %copy-done, f32[2,1024]{1,0:T(2,128)S(1)} %copy-done.1), custom_call_target="tpu_custom_call" | custom-call | flops 13421772800 | bytes 13107200 | tf_op jit(solution)/shard_map/gather_multiply/pallas_call | solution.py:254
  135.7 8.6 %fusion = (f32[2,320,4,2,160]{4,1,0,3,2:T(8,128)}, f32[2,320,4,2,160]{4,1,0,3,2:T(8,128)}) fusion(f32[4,2,2,320,160]{4,3,2,1,0:T(8,128)} %get-tuple-element.7, bf16[4,2,2,320,160]{4,3,2,1,0:T(8,128)(2,1)} %get-tuple-element.8, pred[]{:T(512)S(6)} %eq.4), kind=kLoop, calls=%fused_computation.3 | loop fusion | flops 2457600 | bytes 11468801 | tf_op jit(solution)/shard_map/jit(_where)/select_n | solution.py:285
  144.3 5.7 %copy.3 = f32[2,320,4,2,160]{1,4,3,2,0:T(8,128)} copy(f32[2,320,4,2,160]{4,1,0,3,2:T(8,128)} %get-tuple-element.9) | data formatting | bytes 6553600 | tf_op jit(solution)/shard_map/jit(_where)/select_n | solution.py:285
  150.0 5.7 %copy.4 = f32[2,320,4,2,160]{1,4,3,2,0:T(8,128)} copy(f32[2,320,4,2,160]{4,1,0,3,2:T(8,128)} %get-tuple-element.10) | data formatting | bytes 6553600 | tf_op jit(solution)/shard_map/jit(_where)/select_n | solution.py:286
  155.6 6.9 %pad_maximum_fusion = f32[2,320,2560]{1,2,0:T(8,128)} fusion(f32[2,320,1280]{1,2,0:T(8,128)} %bitcast.7, f32[2,320,1280]{1,2,0:T(8,128)} %bitcast.6), kind=kLoop, calls=%fused_computation | loop fusion | flops 1638400 | bytes 13107200 | tf_op jit(solution)/shard_map/concatenate | solution.py:287
  162.5 8.6 %copy.5 = f32[2,320,2560]{2,1,0:T(8,128)} copy(f32[2,320,2560]{1,2,0:T(8,128)} %pad_maximum_fusion) | data formatting | bytes 13107200 | tf_op jit(solution)/shard_map/concatenate | solution.py:287
Async XLA Ops:
  0.0 1.1 copy-start
  1.1 0.7 copy-start.1

commit v2 on v1

--- a/solution.py
+++ b/solution.py
@@ -7,23 +7,21 @@
 
 MESH = pl.DeviceIdType.MESH
 LAST = (((1,), (1,)), ((), ()))
-XFIRST = (2, 3)
-
-U = lambda j, ms, ts=(0, 1): [("U", j, t, m) for m in ms for t in ts]
-SIDES = lambda ms, ts=(0, 1): [("U", j, t, m) for t in ts for m in ms for j in (3, 1)]
+XFIRST = ((0, 0), (0, 1), (1, 0))
 ORDER = (
-    [("R", "s01"), ("U", 0, 0, 0), ("U", 0, 0, 1), ("R", "12_0"), ("R", "10_1"), ("U", 0, 1, 0), ("U", 0, 1, 1)]
-    + [("U", 3, 0, 0), ("U", 1, 0, 0), ("R", "12_1"), ("R", "10_0"), ("U", 3, 0, 1), ("U", 1, 0, 1)]
-    + [("R", "02"), ("S", 0), ("R", "s11"), ("S", 1), ("R", "s03"), ("R", "s13")]
-    + [("U", 0, 0, 2), ("U", 0, 0, 3), ("U", 0, 1, 2), ("U", 0, 1, 3)]
-    + [("U", 3, 1, 0), ("U", 1, 1, 0), ("U", 3, 1, 1), ("U", 1, 1, 1)]
-    + [("S", 2), ("S", 3)]
-    + [("U", 3, 0, 2), ("U", 1, 0, 2), ("U", 3, 0, 3), ("U", 1, 0, 3)]
-    + [("U", 2, 0, 0), ("U", 2, 1, 0)]
-    + [("U", 3, 1, 2), ("U", 1, 1, 2), ("U", 3, 1, 3), ("U", 1, 1, 3)]
-    + [("U", 2, 0, 1), ("U", 2, 1, 1)]
-    + [("U", 2, 0, 2), ("U", 2, 1, 2), ("U", 2, 0, 3), ("U", 2, 1, 3)]
+    ("R", "s01"), ("U", 0, 1, 0), ("P",), ("U", 0, 0, 1), ("P",), ("U", 0, 1, 1), ("Z", 0, "rest"), ("Z", 0, "root"),
+    ("U", 0, 1, 3), ("U", 0, 1, 2), ("Z", 1, "rest"), ("R", "10_1"), ("Z", 1, "root"), ("U", 0, 0, 0), ("R", "10_0"),
+    ("U", 0, 0, 2), ("U", 3, 1, 3), ("R", "s11"), ("R", "12_0"), ("U", 3, 1, 1), ("U", 0, 0, 3), ("R", "12_1"),
+    ("R", "02"), ("P",), ("U", 1, 1, 0), ("U", 3, 1, 2), ("Y", 1, 1, 0), ("S", 1), ("S", 0), ("U", 3, 0, 0), ("P",),
+    ("P",), ("S", 2), ("R", "s13"), ("Y", 3, 0, 0), ("R", "s03"), ("S", 3), ("U", 1, 0, 0), ("Y", 1, 0, 0), ("P",),
+    ("P",), ("U", 1, 1, 3), ("P",), ("U", 3, 0, 1), ("Y", 3, 0, 1), ("P",), ("U", 3, 1, 0), ("U", 3, 0, 2), ("P",),
+    ("Y", 3, 1, 0), ("U", 1, 1, 1), ("U", 1, 1, 2), ("U", 1, 0, 1), ("P",), ("Y", 1, 0, 1), ("U", 1, 0, 2),
+    ("U", 1, 0, 3), ("U", 2, 0, 0), ("Y", 2, 0, 0), ("P",), ("P",), ("U", 2, 1, 0), ("Y", 2, 1, 0), ("U", 3, 0, 3),
+    ("P",), ("P",), ("P",), ("P",), ("U", 2, 0, 1), ("Y", 2, 0, 1), ("U", 2, 0, 2), ("P",), ("P",), ("P",),
+    ("U", 2, 0, 3), ("U", 2, 1, 1), ("U", 2, 1, 3), ("U", 2, 1, 2),
 )
+
+EARLY = ((2, 0), (2, 1))
 
 
 class Sems:
@@ -34,7 +32,7 @@
         return self.ids.setdefault(name, len(self.ids))
 
 
-def kernel(names, a, f, outl, outr, rows, facs, scaled, cols, acc, snd, sems):
+def kernel(names, a, f, outl, outr, rows, facs, scaled, cols, acc, early, snd, sems):
     p, q = lax.axis_index("panel"), lax.axis_index("pole")
     x, zl, y = lax.rem(p, 4), lax.rem(lax.div(p, 4), 2), lax.div(p, 8)
     zh, c = lax.div(q, 2), lax.rem(q, 2)
@@ -85,19 +83,22 @@
     def sends(j, t, m):
         every = (0, 1, 2, 3)
         out = []
-        xroles = (0,) if m in XFIRST else every
+        xroles = (0,) if (t, m) in XFIRST else every
         if j == 0:
-            out += [(xroles, right, 3), (xroles, left, 1)]
+            out += [(xroles, right, 3, "x"), (xroles, left, 1, "x")]
         elif j == 3 and t == 0:
-            out += [(xroles, right, 2)]
+            out += [(xroles, right, 2, "x")]
         elif j == 1 and t == 1:
-            out += [(xroles, left, 2)]
-        if j == 0 or m in XFIRST:
-            out += [((0, 1), ahead, j), ((0,), behind, j)]
+            out += [(xroles, left, 2, "x")]
+        if j == 0 or (t, m) in XFIRST:
+            out += [((0, 1), ahead, j, "y"), ((0,), behind, j, "y")]
         return out
 
-    def forward(j, t, m):
-        for n, (roles, to, slot) in enumerate(sends(j, t, m)):
+    def forward(j, t, m, axes):
+        for n, (roles, to, slot, axis) in enumerate(sends(j, t, m)):
+            if axis not in axes:
+                continue
+
             def make(root, to=to, slot=slot, n=n):
                 return to_slot(source(j, t, m, root), cols.at[slot, t, m], ("c", j, t, m, n), ("c", slot, t, m), to)
             if j == 0:
@@ -116,13 +117,18 @@
 
     def send_unit(j, t, m):
         if j == 0:
-            def root_local():
+            def at_root():
+                if m >= 2:
+                    wait_rows(0, m, t)
+                if m == 2:
+                    half_to_sibling(t).start()
                 pltpu.make_async_copy(source(0, t, m, True), cols.at[0, t, m], sem(("l", t, m))).start()
-            pl.when(role == 0)(root_local)
+
+            pl.when(role == 0)(at_root)
             pl.when(role != 0)(lambda: wait_unit(j, t, m))
         else:
             wait_unit(j, t, m)
-        forward(j, t, m)
+        forward(j, t, m, ("x",) if ("Y", j, t, m) in ORDER else ("x", "y"))
 
     def wait_rows(w, m, t=None):
         ref = rows.at[w, m] if t is None else part(rows.at[w, m], t)
@@ -132,16 +138,30 @@
     def to_sibling(w, m):
         src = a if (w, m) == (0, 0) else rows.at[w, m]
         start(lambda: to_slot(src, rows.at[w, m + 1], ("w", w, m), ("w", w, m + 1), sibling))
+
+    def half_to_sibling(t):
+        return to_slot(part(rows.at[0, 2], t), part(rows.at[0, 3], t), ("w", 0, 2, t), ("w", 0, 3, t), sibling)
+
+    def is_root(zh, c):
+        return (lax.div(y, 2) == zh) & (lax.rem(y, 2) == c)
+
+    sibling_root, across_root, across2_root = is_root(zh, 1 - c), is_root(1 - zh, c), is_root(1 - zh, 1 - c)
 
     def row_event(kind):
         if kind == "s01":
             wait_rows(0, 1)
         elif kind == "12_0":
             wait_rows(1, 2, 0)
-            start(lambda: to_slot(part(rows.at[1, 2], 0), part(rows.at[0, 2], 0), ("z", 0), ("w", 0, 2, 0), partner))
+            start(
+                lambda: to_slot(part(rows.at[1, 2], 0), part(rows.at[0, 2], 0), ("z", 0), ("w", 0, 2, 0), partner),
+                role != 0,
+            )
         elif kind == "10_1":
             wait_rows(1, 0, 1)
-            start(lambda: to_slot(part(rows.at[1, 0], 1), part(rows.at[0, 2], 1), ("z", 1), ("w", 0, 2, 1), other))
+            start(
+                lambda: to_slot(part(rows.at[1, 0], 1), part(rows.at[0, 2], 1), ("z", 1), ("w", 0, 2, 1), other),
+                jnp.logical_not(across_root),
+            )
         elif kind == "12_1":
             wait_rows(1, 2, 1)
             to_sibling(1, 2)
@@ -149,13 +169,26 @@
             wait_rows(1, 0, 0)
             to_sibling(1, 0)
         elif kind == "02":
-            wait_rows(0, 2, 0)
-            wait_rows(0, 2, 1)
-            to_sibling(0, 2)
+
+            def elsewhere():
+                for t in (0, 1):
+                    wait_rows(0, 2, t)
+
+            pl.when(role != 0)(elsewhere)
+            for t in (0, 1):
+                pl.when((role != 0) & jnp.logical_not(sibling_root))(lambda: half_to_sibling(t).start())
+                finish.append(
+                    lambda t=t: pl.when(jnp.logical_not(sibling_root))(lambda: half_to_sibling(t).wait_send())
+                )
         elif kind == "s11":
             wait_rows(1, 1)
         elif kind == "s03":
-            wait_rows(0, 3)
+
+            def elsewhere():
+                for t in (0, 1):
+                    wait_rows(0, 3, t)
+
+            pl.when(role != 0)(elsewhere)
         elif kind == "s13":
             wait_rows(1, 3)
 
@@ -176,69 +209,90 @@
 
             lax.fori_loop(0, full // step, body, 0)
 
-    def piece(i, j, t, w, e):
-        total = None
-        for m in range(4):
+    def piece(i, j, t, w, e, quarters, first, last):
+        total = None if first else (acc[i, e] if w == 0 else early[i, e])
+        for m in quarters:
             term = lax.dot_general(scaled[m, w * 2 + e], cols[j, t, m], LAST, preferred_element_type=jnp.float32)
             total = term if total is None else total + term
+        if not last:
+            if w:
+                early[i, e] = total
+            else:
+                acc[i, e] = total
+            return
         if w:
             snd[i, e] = total.astype(jnp.bfloat16)
+            column = lax.rem(x + j, 4)
+            start(lambda: to_slot(snd.at[i, e], outr.at[column, t, e], ("o", i, e), ("o", j, t, e), partner))
         else:
             acc[i, e] = total
-        if e == 1:
+        if e == 1 and not w:
             column = lax.rem(x + j, 4)
-            if w:
-                start(lambda: to_slot(snd.at[i], outr.at[column, t], ("o", i), ("o", j, t), partner))
-            else:
-                local = lambda: pltpu.make_async_copy(acc.at[i], outl.at[column, t], sem(("ol", i)))
-                local().start()
-                finish.append(lambda: local().wait())
-
-    def z_start(t, m, to):
-        start(lambda: to_slot(part(a, t), part(rows.at[1, m], t), ("z", m, t), ("w", 1, m, t), to))
-
-    z_start(0, 2, other)
-    z_start(1, 0, partner)
+            local = lambda: pltpu.make_async_copy(acc.at[i], outl.at[column, t], sem(("ol", i)))
+            local().start()
+            finish.append(lambda: local().wait())
+
+    def z_start(turn, where):
+        for t, m, to in ((turn, 2, other), (1 - turn, 0, partner)):
+            make = lambda t=t, m=m, to=to: to_slot(
+                part(a, t), part(rows.at[1, m], t), ("z", m, t), ("w", 1, m, t), to
+            )
+            pl.when((role == 0) if where == "root" else (role != 0))(lambda: make().start())
+            if where == "root":
+                finish.append(lambda make=make: make().wait_send())
+
+    for m, to, when in ((2, across, across_root), (3, across2, across2_root)):
+        for t in (0, 1):
+            make = lambda m=m, to=to, t=t: to_slot(part(a, t), part(rows.at[0, m], t), ("d", m, t), ("w", 0, m, t), to)
+            start(make, when)
     to_sibling(0, 0)
-    z_start(1, 2, other)
-    z_start(0, 0, partner)
     for m, to in ((1, sibling), (2, across), (3, across2)):
         start(lambda m=m, to=to: to_slot(f, facs.at[m], ("f", m), ("f", m), to))
 
-    pending, seen, done = [], {}, 0
-    scaled_ready = 0
-    ready = []
+    pending, seen, number, ready, scales = [], {}, {}, [], 0
     for event in ORDER:
         if event[0] == "R":
             row_event(event[1])
+        elif event[0] == "Z":
+            z_start(*event[1:])
+        elif event[0] == "Y":
+            forward(*event[1:], ("y",))
         elif event[0] == "S":
             scale(event[1])
-            scaled_ready += 1
-        else:
+            scales += 1
+        elif event[0] == "U":
             _, j, t, m = event
             send_unit(j, t, m)
-            seen[j, t] = seen.get((j, t), 0) + 1
-            if seen[j, t] == 4:
-                ready.append((j, t))
-        if scaled_ready == 4:
-            while ready:
-                j, t = ready.pop(0)
-                if j == 0:
-                    for m in range(4):
-                        pl.when(role == 0)(
-                            lambda: pltpu.make_async_copy(source(0, t, m, True), cols.at[0, t, m], sem(("l", t, m))).wait()
-                        )
-                pending += [(done, j, t, w, e) for w in (1, 0) for e in (0, 1)]
-                done += 1
-            if pending:
-                piece(*pending.pop(0))
+            got = seen.setdefault((j, t), [])
+            got.append(m)
+            if (j, t) in EARLY:
+                if len(got) == 3:
+                    ready.append((j, t, tuple(got), True, False))
+                elif len(got) == 4:
+                    ready.append((j, t, (m,), False, True))
+            elif len(got) == 4:
+                ready.append((j, t, (0, 1, 2, 3), True, True))
+        if event[0] in ("Y", "Z") or scales < 4:
+            continue
+        while ready:
+            j, t, quarters, first, last = ready.pop(0)
+            if j == 0:
+                for m in range(4):
+                    pl.when(role == 0)(
+                        lambda: pltpu.make_async_copy(source(0, t, m, True), cols.at[0, t, m], sem(("l", t, m))).wait()
+                    )
+            i = number.setdefault((j, t), len(number))
+            pending += [(i, j, t, w, e, quarters, first, last) for w in (1, 0) for e in (0, 1)]
+        if pending:
+            piece(*pending.pop(0))
     while pending:
         piece(*pending.pop(0))
 
     for j in range(4):
         for t in (0, 1):
             column = lax.rem(x + j, 4)
-            to_slot(snd.at[0], outr.at[column, t], ("o", 0), ("o", j, t), partner).wait_recv()
+            for e in (0, 1):
+                to_slot(snd.at[0, e], outr.at[column, t, e], ("o", 0, e), ("o", j, t, e), partner).wait_recv()
     for wait in finish:
         wait()
 
@@ -262,6 +316,7 @@
             pltpu.VMEM((4, 4, n, k), bf16),
             pltpu.VMEM((4, 2, 4, half, k), bf16),
             pltpu.VMEM((8, 2, n, half), f32),
+            pltpu.VMEM((8, 2, n, half), f32),
             pltpu.VMEM((8, 2, n, half), bf16),
             pltpu.SemaphoreType.DMA((256,)),
         ],
@@ -273,18 +328,31 @@
     )(a, f)
 
 
+def assemble_kernel(mine, theirs, out):
+    zl = lax.rem(lax.div(lax.axis_index("panel"), 4), 2)
+    width = out.shape[2] // 2
+    for block, at in ((mine, zl), (theirs, 1 - zl)):
+        pieces = [block[x, t, 0].astype(jnp.float32) for x in range(4) for t in range(2)]
+        out[0, :, pl.ds(pl.multiple_of(at * width, 128), width)] = jnp.concatenate(pieces, axis=1)
+
+
+def assemble(mine, theirs):
+    _, _, energies, n, half = mine.shape
+    step = 80
+    block = pl.BlockSpec((4, 2, 1, step, half), lambda e, i: (0, 0, e, i, 0))
+    return pl.pallas_call(
+        assemble_kernel,
+        out_shape=jax.ShapeDtypeStruct((energies, n, 16 * half), jnp.float32),
+        grid=(energies, n // step),
+        in_specs=[block, block],
+        out_specs=pl.BlockSpec((1, step, 16 * half), lambda e, i: (e, i, 0)),
+        compiler_params=pltpu.CompilerParams(vmem_limit_bytes=56 << 20),
+        name="assemble",
+    )(mine, theirs)
+
+
 def shards(a, f):
-    n = a.shape[0]
-    zl = lax.rem(lax.div(lax.axis_index("panel"), 4), 2)
-    mine, theirs = gather_and_multiply(a, f)
-
-    def flat(block):
-        return jnp.transpose(block, (2, 3, 0, 1, 4)).reshape(2, n, 4 * n)
-
-    mine, theirs = flat(mine), flat(theirs).astype(jnp.float32)
-    first = jnp.where(zl == 0, mine, theirs)
-    second = jnp.where(zl == 0, theirs, mine)
-    return jnp.concatenate([first, second], axis=2)
+    return assemble(*gather_and_multiply(a, f))
 
 
 def solution(mesh):

time: 172 us -> 130 us (0.76)
  local copies, waits for them, and re-layouts: 21.7 us -> 1.78 us
  other arithmetic: 15.5 us -> 0 us
  Pallas kernels: 134 us -> 127 us
    pallas_call x1, Pallas kernels: 134 us -> 119 us  [gather_and_multiply(): pl.pallas_call(lambda *refs: kernel(names, *refs), out_shape=(jax.ShapeDt...]
    select_n x2 -> x0, local copies, waits for them, and re-layouts: 11.3 us -> none  [the longest x1 5.67 us: shards(): first = jnp.where(zl == 0, mine, theirs)]
    pallas_call x0 -> x1, Pallas kernels: none -> 8.84 us  [assemble(): pl.pallas_call(assemble_kernel, out_shape=jax.ShapeDtypeStruct((energies,...]
    select_n x1 -> x0, other arithmetic: 8.63 us -> none  [shards(): first = jnp.where(zl == 0, mine, theirs)]
    concatenate x1 -> x0, local copies, waits for them, and re-layouts: 8.56 us -> none  [shards(): return jnp.concatenate([first, second], axis=2)]
    concatenate x1 -> x0, other arithmetic: 6.89 us -> none  [shards(): return jnp.concatenate([first, second], axis=2)]
where the time goes in v2:
time: 130 us; the launch traced here: 129 us
  Pallas kernels  127 us (98%)
  local copies, waits for them, and re-layouts  1.78 us (1%)
    pallas_call x1, Pallas kernels, gather_and_multiply(): pl.pallas_call(lambda *refs: kernel(names, *refs), out_shape=(jax.ShapeDt...  119 us
    pallas_call x1, Pallas kernels, assemble(): pl.pallas_call(assemble_kernel, out_shape=jax.ShapeDtypeStruct((energies,...  8.84 us

profile of v2, /device:TPU:16, one launch (start us, length us, event | category | flops | bytes accessed | tf_op | source)
XLA Modules:
  0.0 129.3 jit_solution(7045865965998929798)
XLA Ops:
  0.0 0.0 copy-start
  0.0 1.1 copy-done
  1.1 0.0 copy-start.1
  1.1 0.7 copy-done.1
  1.8 118.6 %gather_multiply.1 = (f32[4,2,2,320,160]{4,3,2,1,0:T(8,128)}, bf16[4,2,2,320,160]{4,3,2,1,0:T(8,128)(2,1)}) custom-call(bf16[320,1024]{1,0:T(8,128)(2,1)S(1)} %copy-done, f32[2,1024]{1,0:T(2,128)S(1)} %copy-done.1), custom_call_target="tpu_custom_call" | custom-call | flops 13421772800 | bytes 13107200 | tf_op jit(solution)/shard_map/gather_multiply/pallas_call | solution.py:308
  120.4 8.8 %assemble.1 = f32[2,320,2560]{2,1,0:T(8,128)} custom-call(f32[4,2,2,320,160]{4,3,2,1,0:T(8,128)} %get-tuple-element.7.mine, bf16[4,2,2,320,160]{4,3,2,1,0:T(8,128)(2,1)} %get-tuple-element.8.theirs), custom_call_target="tpu_custom_call" | custom-call | tf_op jit(solution)/shard_map/assemble/pallas_call | solution.py:343
Async XLA Ops:
  0.0 1.1 copy-start
  1.1 0.7 copy-start.1

commit v3 on v2

--- a/solution.py
+++ b/solution.py
@@ -7,18 +7,18 @@
 
 MESH = pl.DeviceIdType.MESH
 LAST = (((1,), (1,)), ((), ()))
-XFIRST = ((0, 0), (0, 1), (1, 0))
+XFIRST = ((0, 1), (1, 1), (1, 3))
 ORDER = (
-    ("R", "s01"), ("U", 0, 1, 0), ("P",), ("U", 0, 0, 1), ("P",), ("U", 0, 1, 1), ("Z", 0, "rest"), ("Z", 0, "root"),
-    ("U", 0, 1, 3), ("U", 0, 1, 2), ("Z", 1, "rest"), ("R", "10_1"), ("Z", 1, "root"), ("U", 0, 0, 0), ("R", "10_0"),
-    ("U", 0, 0, 2), ("U", 3, 1, 3), ("R", "s11"), ("R", "12_0"), ("U", 3, 1, 1), ("U", 0, 0, 3), ("R", "12_1"),
-    ("R", "02"), ("P",), ("U", 1, 1, 0), ("U", 3, 1, 2), ("Y", 1, 1, 0), ("S", 1), ("S", 0), ("U", 3, 0, 0), ("P",),
-    ("P",), ("S", 2), ("R", "s13"), ("Y", 3, 0, 0), ("R", "s03"), ("S", 3), ("U", 1, 0, 0), ("Y", 1, 0, 0), ("P",),
-    ("P",), ("U", 1, 1, 3), ("P",), ("U", 3, 0, 1), ("Y", 3, 0, 1), ("P",), ("U", 3, 1, 0), ("U", 3, 0, 2), ("P",),
-    ("Y", 3, 1, 0), ("U", 1, 1, 1), ("U", 1, 1, 2), ("U", 1, 0, 1), ("P",), ("Y", 1, 0, 1), ("U", 1, 0, 2),
-    ("U", 1, 0, 3), ("U", 2, 0, 0), ("Y", 2, 0, 0), ("P",), ("P",), ("U", 2, 1, 0), ("Y", 2, 1, 0), ("U", 3, 0, 3),
-    ("P",), ("P",), ("P",), ("P",), ("U", 2, 0, 1), ("Y", 2, 0, 1), ("U", 2, 0, 2), ("P",), ("P",), ("P",),
-    ("U", 2, 0, 3), ("U", 2, 1, 1), ("U", 2, 1, 3), ("U", 2, 1, 2),
+    ("R", "s01"), ("U", 0, 0, 0), ("P",), ("Z", 0, "rest"), ("U", 0, 1, 1), ("U", 0, 0, 1), ("P",), ("P",),
+    ("U", 1, 1, 1), ("Z", 1, "rest"), ("U", 0, 1, 3), ("Z", 0, "root"), ("P",), ("Z", 1, "root"), ("U", 3, 1, 1),
+    ("U", 3, 0, 0), ("U", 0, 1, 0), ("P",), ("U", 1, 0, 0), ("U", 0, 1, 2), ("U", 0, 0, 3), ("U", 2, 0, 0),
+    ("Y", 1, 0, 0), ("R", "10"), ("R", "12"), ("R", "02"), ("U", 3, 1, 0), ("S", 0), ("U", 0, 0, 2), ("S", 2),
+    ("R", "s11"), ("S", 1), ("U", 1, 1, 2), ("R", "s13"), ("R", "s03"), ("S", 3), ("U", 1, 1, 0), ("U", 3, 1, 2),
+    ("P",), ("U", 3, 0, 1), ("Y", 3, 0, 1), ("P",), ("P",), ("Y", 3, 1, 0), ("P",), ("Y", 1, 1, 0), ("U", 1, 0, 3),
+    ("U", 3, 1, 3), ("P",), ("Y", 2, 0, 0), ("P",), ("U", 3, 0, 3), ("U", 1, 1, 3), ("U", 1, 0, 2), ("Y", 3, 0, 0),
+    ("P",), ("P",), ("U", 1, 0, 1), ("Y", 1, 0, 1), ("P",), ("P",), ("P",), ("U", 3, 0, 2), ("U", 2, 1, 2),
+    ("U", 2, 1, 1), ("P",), ("U", 2, 1, 0), ("P",), ("U", 2, 0, 1), ("Y", 2, 0, 1), ("P",), ("U", 2, 0, 3), ("P",),
+    ("U", 2, 1, 3), ("Y", 2, 1, 0), ("U", 2, 0, 2),
 )
 
 EARLY = ((2, 0), (2, 1))
@@ -30,6 +30,21 @@
 
     def __getitem__(self, name):
         return self.ids.setdefault(name, len(self.ids))
+
+
+def pack(block, ref):
+    n, width = block.shape
+    groups = 128 // (width - 128)
+    step = n // groups
+    ref[pl.ds(0, n), :] = block[:, :128].astype(ref.dtype)
+    rest = [block[g * step : (g + 1) * step, 128:] for g in range(groups)]
+    ref[pl.ds(n, step), :] = jnp.concatenate(rest, axis=1).astype(ref.dtype)
+
+
+def unpack(block, n, width):
+    rest = width - 128
+    tail = [block[n:, g * rest : (g + 1) * rest] for g in range(128 // rest)]
+    return jnp.concatenate([block[:n], jnp.concatenate(tail, axis=0)], axis=1)
 
 
 def kernel(names, a, f, outl, outr, rows, facs, scaled, cols, acc, early, snd, sems):
@@ -150,23 +165,11 @@
     def row_event(kind):
         if kind == "s01":
             wait_rows(0, 1)
-        elif kind == "12_0":
-            wait_rows(1, 2, 0)
-            start(
-                lambda: to_slot(part(rows.at[1, 2], 0), part(rows.at[0, 2], 0), ("z", 0), ("w", 0, 2, 0), partner),
-                role != 0,
-            )
-        elif kind == "10_1":
-            wait_rows(1, 0, 1)
-            start(
-                lambda: to_slot(part(rows.at[1, 0], 1), part(rows.at[0, 2], 1), ("z", 1), ("w", 0, 2, 1), other),
-                jnp.logical_not(across_root),
-            )
-        elif kind == "12_1":
-            wait_rows(1, 2, 1)
+        elif kind == "12":
+            wait_rows(1, 2)
             to_sibling(1, 2)
-        elif kind == "10_0":
-            wait_rows(1, 0, 0)
+        elif kind == "10":
+            wait_rows(1, 0)
             to_sibling(1, 0)
         elif kind == "02":
 
@@ -195,10 +198,13 @@
     def scale(m):
         if m:
             to_slot(facs.at[m], facs.at[m], ("c", 0, 0, 0, 0), ("f", m), sibling).wait_recv()
-        fac = f if m == 0 else facs.at[m]
+        else:
+            for local in own:
+                local().wait()
+        fac = facs.at[m]
         energies, full, step = f.shape[0], 2 * half, 32
         for w in (0, 1):
-            src = a if (w, m) == (0, 0) else rows.at[w, m]
+            src = rows.at[w, m]
 
             def body(i, _):
                 at = pl.ds(pl.multiple_of(i * step, step), step)
@@ -210,41 +216,51 @@
             lax.fori_loop(0, full // step, body, 0)
 
     def piece(i, j, t, w, e, quarters, first, last):
-        total = None if first else (acc[i, e] if w == 0 else early[i, e])
+        total = None if first else early[EARLY.index((j, t)), w, e]
         for m in quarters:
             term = lax.dot_general(scaled[m, w * 2 + e], cols[j, t, m], LAST, preferred_element_type=jnp.float32)
             total = term if total is None else total + term
         if not last:
-            if w:
-                early[i, e] = total
-            else:
-                acc[i, e] = total
+            early[EARLY.index((j, t)), w, e] = total
             return
+        pack(total, snd.at[i, e] if w else acc.at[i, e])
         if w:
-            snd[i, e] = total.astype(jnp.bfloat16)
             column = lax.rem(x + j, 4)
             start(lambda: to_slot(snd.at[i, e], outr.at[column, t, e], ("o", i, e), ("o", j, t, e), partner))
-        else:
-            acc[i, e] = total
-        if e == 1 and not w:
+        elif e == 1:
             column = lax.rem(x + j, 4)
             local = lambda: pltpu.make_async_copy(acc.at[i], outl.at[column, t], sem(("ol", i)))
             local().start()
             finish.append(lambda: local().wait())
 
+    own = (
+        lambda: pltpu.make_async_copy(a, rows.at[0, 0], sem(("own", 0))),
+        lambda: pltpu.make_async_copy(f, facs.at[0], sem(("own", 1))),
+    )
+    for local in own:
+        local().start()
+    def far(m, t, to):
+        return to_slot(part(a, t), part(rows.at[0, m], t), ("d", m, t), ("w", 0, m, t), to)
+
     def z_start(turn, where):
-        for t, m, to in ((turn, 2, other), (1 - turn, 0, partner)):
-            make = lambda t=t, m=m, to=to: to_slot(
-                part(a, t), part(rows.at[1, m], t), ("z", m, t), ("w", 1, m, t), to
-            )
-            pl.when((role == 0) if where == "root" else (role != 0))(lambda: make().start())
+        here = (role == 0) if where == "root" else (role != 0)
+        if turn == 0:
+            makes = [
+                lambda m=m, to=to: to_slot(a, rows.at[1, m], ("z", m), ("w", 1, m), to)
+                for m, to in ((2, other), (0, partner))
+            ]
+        else:
+            makes = [lambda t=t: far(2, t, across) for t in (0, 1)]
+            here = here & jnp.logical_not(across_root)
+        for make in makes:
+            pl.when(here)(lambda: make().start())
             if where == "root":
                 finish.append(lambda make=make: make().wait_send())
 
-    for m, to, when in ((2, across, across_root), (3, across2, across2_root)):
-        for t in (0, 1):
-            make = lambda m=m, to=to, t=t: to_slot(part(a, t), part(rows.at[0, m], t), ("d", m, t), ("w", 0, m, t), to)
-            start(make, when)
+    for t in (0, 1):
+        pl.when(across_root)(lambda: far(2, t, across).start())
+    for t in (0, 1):
+        start(lambda t=t: far(3, t, across2), across2_root)
     to_sibling(0, 0)
     for m, to in ((1, sibling), (2, across), (3, across2)):
         start(lambda m=m, to=to: to_slot(f, facs.at[m], ("f", m), ("f", m), to))
@@ -301,58 +317,82 @@
     n, k = a.shape
     half = n // 2
     names = Sems()
-    shape = (4, 2, 2, n, half)
+    shape = (4, 2, 2, n * half // 128, 128)
     bf16, f32 = jnp.bfloat16, jnp.float32
     any_ = pl.BlockSpec(memory_space=pl.ANY)
-    vmem = pl.BlockSpec(memory_space=pltpu.VMEM)
     return pl.pallas_call(
         lambda *refs: kernel(names, *refs),
         out_shape=(jax.ShapeDtypeStruct(shape, f32), jax.ShapeDtypeStruct(shape, bf16)),
-        in_specs=[vmem, vmem],
+        in_specs=[any_, any_],
         out_specs=(any_, any_),
         scratch_shapes=[
             pltpu.VMEM((2, 4, n, k), bf16),
             pltpu.VMEM((4, 2, k), f32),
             pltpu.VMEM((4, 4, n, k), bf16),
             pltpu.VMEM((4, 2, 4, half, k), bf16),
-            pltpu.VMEM((8, 2, n, half), f32),
-            pltpu.VMEM((8, 2, n, half), f32),
-            pltpu.VMEM((8, 2, n, half), bf16),
+            pltpu.VMEM((8,) + shape[2:], f32),
+            pltpu.VMEM((len(EARLY), 2, 2, n, half), f32),
+            pltpu.VMEM((8,) + shape[2:], bf16),
             pltpu.SemaphoreType.DMA((256,)),
         ],
         compiler_params=pltpu.CompilerParams(
-            collective_id=0, has_side_effects=True, vmem_limit_bytes=52 << 20
+            collective_id=0, has_side_effects=True, vmem_limit_bytes=60 << 20
         ),
         cost_estimate=pl.CostEstimate(flops=2 * 4 * n * 8 * half * 4 * k, bytes_accessed=8 * n * n * 16, transcendentals=0),
         name="gather_multiply",
     )(a, f)
 
 
-def assemble_kernel(mine, theirs, out):
+def assemble_kernel(n, width, mine, theirs, out, mine_in, theirs_in, blocks, in_sems, out_sems):
     zl = lax.rem(lax.div(lax.axis_index("panel"), 4), 2)
-    width = out.shape[2] // 2
-    for block, at in ((mine, zl), (theirs, 1 - zl)):
-        pieces = [block[x, t, 0].astype(jnp.float32) for x in range(4) for t in range(2)]
-        out[0, :, pl.ds(pl.multiple_of(at * width, 128), width)] = jnp.concatenate(pieces, axis=1)
-
-
-def assemble(mine, theirs):
-    _, _, energies, n, half = mine.shape
-    step = 80
-    block = pl.BlockSpec((4, 2, 1, step, half), lambda e, i: (0, 0, e, i, 0))
+    turns = [(e, pair, kind) for e in (0, 1) for pair in (0, 1) for kind in (0, 1)]
+
+    def fetch(i):
+        e, pair, kind = turns[i]
+        src, dst = (mine, mine_in) if kind == 0 else (theirs, theirs_in)
+        at = pl.ds(2 * pair, 2)
+        return pltpu.make_async_copy(src.at[at, :, e], dst.at[e, pair], in_sems.at[i])
+
+    def leave(i):
+        e, pair, kind = turns[i]
+        side = zl if kind == 0 else 1 - zl
+        at = pl.ds(pl.multiple_of((side * 2 + pair) * 4 * width, 128), 4 * width)
+        return pltpu.make_async_copy(blocks.at[i], out.at[e, :, at], out_sems.at[i])
+
+    for i in range(len(turns)):
+        fetch(i).start()
+    for i, (e, pair, kind) in enumerate(turns):
+        fetch(i).wait()
+        block = (mine_in if kind == 0 else theirs_in).at[e, pair]
+        pieces = [unpack(block[x, t].astype(jnp.float32), n, width) for x in (0, 1) for t in (0, 1)]
+        blocks[i] = jnp.concatenate(pieces, axis=1)
+        leave(i).start()
+    for i in range(len(turns)):
+        leave(i).wait()
+
+
+def assemble(mine, theirs, n, width):
+    any_ = pl.BlockSpec(memory_space=pl.ANY)
+    block = (2, 2, 2, 2) + mine.shape[3:]
     return pl.pallas_call(
-        assemble_kernel,
-        out_shape=jax.ShapeDtypeStruct((energies, n, 16 * half), jnp.float32),
-        grid=(energies, n // step),
-        in_specs=[block, block],
-        out_specs=pl.BlockSpec((1, step, 16 * half), lambda e, i: (e, i, 0)),
+        lambda *refs: assemble_kernel(n, width, *refs),
+        out_shape=jax.ShapeDtypeStruct((2, n, 16 * width), jnp.float32),
+        in_specs=[any_, any_],
+        out_specs=any_,
+        scratch_shapes=[
+            pltpu.VMEM(block, jnp.float32),
+            pltpu.VMEM(block, jnp.bfloat16),
+            pltpu.VMEM((8, n, 4 * width), jnp.float32),
+            pltpu.SemaphoreType.DMA((8,)),
+            pltpu.SemaphoreType.DMA((8,)),
+        ],
         compiler_params=pltpu.CompilerParams(vmem_limit_bytes=56 << 20),
         name="assemble",
     )(mine, theirs)
 
 
 def shards(a, f):
-    return assemble(*gather_and_multiply(a, f))
+    return assemble(*gather_and_multiply(a, f), a.shape[0], a.shape[0] // 2)
 
 
 def solution(mesh):

time: 130 us -> 112 us (0.86)
  Pallas kernels: 127 us -> 111 us
  local copies, waits for them, and re-layouts: 1.78 us -> 0 us
    pallas_call x1, Pallas kernels: 119 us -> 106 us  [gather_and_multiply(): pl.pallas_call(lambda *refs: kernel(names, *refs), out_shape=(jax.ShapeDt...]
    pallas_call x1, Pallas kernels: 8.84 us -> 4.9 us  [assemble(): pl.pallas_call(lambda *refs: assemble_kernel(n, width, *refs), out_shape=...]
    unnamed x4 -> x0, local copies, waits for them, and re-layouts: 1.78 us -> none
where the time goes in v3:
time: 112 us; the launch traced here: 111 us
  Pallas kernels  111 us (99%)
    pallas_call x1, Pallas kernels, gather_and_multiply(): pl.pallas_call(lambda *refs: kernel(names, *refs), out_shape=(jax.ShapeDt...  106 us
    pallas_call x1, Pallas kernels, assemble(): pl.pallas_call(lambda *refs: assemble_kernel(n, width, *refs), out_shape=...  4.9 us

profile of v3, /device:TPU:16, one launch (start us, length us, event | category | flops | bytes accessed | tf_op | source)
XLA Modules:
  0.0 111.4 jit_solution(3730992798482320989)
XLA Ops:
  0.0 106.4 %gather_multiply.1 = (f32[4,2,2,400,128]{4,3,2,1,0:T(8,128)}, bf16[4,2,2,400,128]{4,3,2,1,0:T(8,128)(2,1)}) custom-call(bf16[320,1024]{1,0:T(8,128)(2,1)} %refs_0_.1, f32[2,1024]{1,0:T(2,128)} %refs_1_.1), custom_call_target="tpu_custom_call" | custom-call | flops 13421772800 | bytes 13107200 | tf_op jit(solution)/shard_map/gather_multiply/pallas_call | solution.py:323
  106.4 4.9 %assemble.1 = f32[2,320,2560]{2,1,0:T(8,128)} custom-call(f32[4,2,2,400,128]{4,3,2,1,0:T(8,128)} %get-tuple-element.7.refs_0_, bf16[4,2,2,400,128]{4,3,2,1,0:T(8,128)(2,1)} %get-tuple-element.8.refs_1_), custom_call_target="tpu_custom_call" | custom-call | tf_op jit(solution)/shard_map/assemble/pallas_call | solution.py:377

commit v4 on v3

--- a/solution.py
+++ b/solution.py
@@ -7,18 +7,18 @@
 
 MESH = pl.DeviceIdType.MESH
 LAST = (((1,), (1,)), ((), ()))
-XFIRST = ((0, 1), (1, 1), (1, 3))
+XFIRST = ((1, 1), (1, 2), (1, 3))
 ORDER = (
-    ("R", "s01"), ("U", 0, 0, 0), ("P",), ("Z", 0, "rest"), ("U", 0, 1, 1), ("U", 0, 0, 1), ("P",), ("P",),
-    ("U", 1, 1, 1), ("Z", 1, "rest"), ("U", 0, 1, 3), ("Z", 0, "root"), ("P",), ("Z", 1, "root"), ("U", 3, 1, 1),
-    ("U", 3, 0, 0), ("U", 0, 1, 0), ("P",), ("U", 1, 0, 0), ("U", 0, 1, 2), ("U", 0, 0, 3), ("U", 2, 0, 0),
-    ("Y", 1, 0, 0), ("R", "10"), ("R", "12"), ("R", "02"), ("U", 3, 1, 0), ("S", 0), ("U", 0, 0, 2), ("S", 2),
-    ("R", "s11"), ("S", 1), ("U", 1, 1, 2), ("R", "s13"), ("R", "s03"), ("S", 3), ("U", 1, 1, 0), ("U", 3, 1, 2),
-    ("P",), ("U", 3, 0, 1), ("Y", 3, 0, 1), ("P",), ("P",), ("Y", 3, 1, 0), ("P",), ("Y", 1, 1, 0), ("U", 1, 0, 3),
-    ("U", 3, 1, 3), ("P",), ("Y", 2, 0, 0), ("P",), ("U", 3, 0, 3), ("U", 1, 1, 3), ("U", 1, 0, 2), ("Y", 3, 0, 0),
-    ("P",), ("P",), ("U", 1, 0, 1), ("Y", 1, 0, 1), ("P",), ("P",), ("P",), ("U", 3, 0, 2), ("U", 2, 1, 2),
-    ("U", 2, 1, 1), ("P",), ("U", 2, 1, 0), ("P",), ("U", 2, 0, 1), ("Y", 2, 0, 1), ("P",), ("U", 2, 0, 3), ("P",),
-    ("U", 2, 1, 3), ("Y", 2, 1, 0), ("U", 2, 0, 2),
+    ("R", "s01"), ("U", 0, 0, 0), ("Z", 0, "far"), ("Z", 1, "far"), ("Z", 0, "root"), ("U", 0, 1, 0),
+    ("Z", 0, "side"), ("U", 0, 1, 1), ("U", 1, 0, 0), ("Z", 1, "side"), ("P",), ("Y", 1, 0, 0), ("U", 0, 1, 2),
+    ("U", 0, 1, 3), ("R", "10"), ("Z", 1, "root"), ("U", 0, 0, 1), ("U", 0, 0, 2), ("U", 0, 0, 3), ("P",), ("P",),
+    ("R", "12"), ("R", "02"), ("U", 3, 1, 2), ("U", 3, 0, 1), ("P",), ("R", "s03"), ("P",), ("U", 1, 1, 0), ("P",),
+    ("S", 2), ("S", 0), ("U", 3, 1, 0), ("Y", 1, 1, 0), ("P",), ("P",), ("R", "s11"), ("S", 1), ("Y", 3, 0, 1),
+    ("R", "s13"), ("U", 3, 1, 1), ("S", 3), ("U", 1, 0, 2), ("U", 1, 0, 1), ("P",), ("U", 1, 1, 2), ("P",), ("P",),
+    ("U", 1, 0, 3), ("U", 1, 1, 3), ("P",), ("U", 3, 0, 0), ("P",), ("U", 3, 1, 3), ("Y", 1, 0, 1), ("Y", 3, 0, 0),
+    ("P",), ("U", 2, 1, 0), ("P",), ("U", 1, 1, 1), ("P",), ("Y", 3, 1, 0), ("U", 3, 0, 3), ("U", 3, 0, 2),
+    ("U", 2, 1, 2), ("Y", 2, 1, 0), ("P",), ("U", 2, 0, 0), ("U", 2, 0, 1), ("Y", 2, 0, 0), ("U", 2, 1, 3), ("P",),
+    ("P",), ("P",), ("U", 2, 0, 3), ("U", 2, 1, 1), ("Y", 2, 0, 1), ("U", 2, 0, 2),
 )
 
 EARLY = ((2, 0), (2, 1))
@@ -243,7 +243,7 @@
         return to_slot(part(a, t), part(rows.at[0, m], t), ("d", m, t), ("w", 0, m, t), to)
 
     def z_start(turn, where):
-        here = (role == 0) if where == "root" else (role != 0)
+        here = {"root": role == 0, "side": role == 3, "far": (role == 1) | (role == 2)}[where]
         if turn == 0:
             makes = [
                 lambda m=m, to=to: to_slot(a, rows.at[1, m], ("z", m), ("w", 1, m), to)
@@ -264,6 +264,10 @@
     to_sibling(0, 0)
     for m, to in ((1, sibling), (2, across), (3, across2)):
         start(lambda m=m, to=to: to_slot(f, facs.at[m], ("f", m), ("f", m), to))
+
+    def next_piece():
+        at = next((n for n, p in enumerate(pending) if p[3] == 1), 0)
+        piece(*pending.pop(at))
 
     pending, seen, number, ready, scales = [], {}, {}, [], 0
     for event in ORDER:
@@ -300,9 +304,9 @@
             i = number.setdefault((j, t), len(number))
             pending += [(i, j, t, w, e, quarters, first, last) for w in (1, 0) for e in (0, 1)]
         if pending:
-            piece(*pending.pop(0))
+            next_piece()
     while pending:
-        piece(*pending.pop(0))
+        next_piece()
 
     for j in range(4):
         for t in (0, 1):

time: 112 us -> 111 us (level)
    pallas_call x1, Pallas kernels: 106 us -> 105 us  [gather_and_multiply(): pl.pallas_call(lambda *refs: kernel(names, *refs), out_shape=(jax.ShapeDt...]
where the time goes in v4:
time: 111 us; the launch traced here: 110 us
  Pallas kernels  110 us (99%)
    pallas_call x1, Pallas kernels, gather_and_multiply(): pl.pallas_call(lambda *refs: kernel(names, *refs), out_shape=(jax.ShapeDt...  105 us
    pallas_call x1, Pallas kernels, assemble(): pl.pallas_call(lambda *refs: assemble_kernel(n, width, *refs), out_shape=...  4.9 us

profile of v4, /device:TPU:16, one launch (start us, length us, event | category | flops | bytes accessed | tf_op | source)
XLA Modules:
  0.0 109.9 jit_solution(13775903717493337021)
XLA Ops:
  0.0 104.8 %gather_multiply.1 = (f32[4,2,2,400,128]{4,3,2,1,0:T(8,128)}, bf16[4,2,2,400,128]{4,3,2,1,0:T(8,128)(2,1)}) custom-call(bf16[320,1024]{1,0:T(8,128)(2,1)} %refs_0_.1, f32[2,1024]{1,0:T(2,128)} %refs_1_.1), custom_call_target="tpu_custom_call" | custom-call | flops 13421772800 | bytes 13107200 | tf_op jit(solution)/shard_map/gather_multiply/pallas_call | solution.py:327
  104.8 4.9 %assemble.1 = f32[2,320,2560]{2,1,0:T(8,128)} custom-call(f32[4,2,2,400,128]{4,3,2,1,0:T(8,128)} %get-tuple-element.7.refs_0_, bf16[4,2,2,400,128]{4,3,2,1,0:T(8,128)(2,1)} %get-tuple-element.8.refs_1_), custom_call_target="tpu_custom_call" | custom-call | tf_op jit(solution)/shard_map/assemble/pallas_call | solution.py:381
